TPU v7x, 32 devices: a whole 2x2x4 slice. The times are simulated.
32 devices in a mesh: prow: 16 (over z, y, core), pcol: 2 (over x).
Axes of the slice: x: 2, y: 2, z: 4, core: 2. Of those that a mesh axis runs over, the one named last changes fastest.
Arguments:
- prior_panel: bfloat16 [16384, 12288], P('prow', 'pcol'), may hold values from -0.0546875 to 0.0546875
- prior_solution: bfloat16 [12288, 256], P('pcol', 'prow'), may hold values from -6 to 6
- right_side: bfloat16 [16384, 256], P('prow', 'pcol'), may hold values from -6 to 6
- new_panel: bfloat16 [2, 16384, 512], P(None, 'prow', 'pcol'), may hold values from -0.25 to 0.25
- inverses: bfloat16 [2, 512, 512], P(None, 'pcol'), as said below
Outputs:
- solved: bfloat16 [2, 512, 256], P(None, 'pcol')
- pending: float32 [16384, 256], P('prow', 'pcol')
Inputs may be any that keep to these rules, and one draw needn't show every extreme that they name: `inverses`: each of the two inverse blocks is lower triangular with a positive diagonal.
All inputs are finite; a program needn't handle non-finite values.
Results may differ from a plain program's by a relative error of at most 0.0057.
Values may be sent and summed in bfloat16 or wider, within the bound.
A program may use at most 64 MiB of HBM per device.

v0:
```python
import jax
import jax.numpy as jnp
from jax import lax
from jax.sharding import PartitionSpec as P


def spread(block, axis, owner):
    block = jnp.where(lax.axis_index(axis) == owner, block, jnp.zeros_like(block))
    return lax.psum(block, axis)


def body(prior_panel, prior_solution, right_side, new_panel, inverses):
    local_rows = prior_panel.shape[0]
    block_size = inverses.shape[2]
    pair_rows = 2 * block_size
    partial_value = jnp.dot(
        prior_panel,
        lax.all_gather(prior_solution, "prow", axis=1, tiled=True),
        preferred_element_type=jnp.float32,
    )
    row_ids = lax.axis_index("prow") * local_rows + lax.iota(jnp.int32, local_rows)
    first_panel = jnp.where(
        (row_ids >= block_size)[:, None], new_panel[0], jnp.zeros_like(new_panel[0])
    )
    second_panel = jnp.where(
        (row_ids >= pair_rows)[:, None], new_panel[1], jnp.zeros_like(new_panel[1])
    )
    pending = right_side.astype(jnp.float32) - lax.psum_scatter(
        partial_value, "pcol", scatter_dimension=1, tiled=True
    )
    solved_list = []
    for section, masked in ((0, first_panel), (1, second_panel)):
        diagonal = pending[section * block_size : (section + 1) * block_size].astype(jnp.bfloat16)
        gathered = lax.all_gather(diagonal, "pcol", axis=1, tiled=True)
        result = spread(
            jnp.dot(inverses[section], gathered, preferred_element_type=jnp.float32).astype(
                jnp.bfloat16
            ),
            "prow",
            0,
        )
        update = jnp.dot(masked, result, preferred_element_type=jnp.float32)
        pending = pending - lax.psum_scatter(update, "pcol", scatter_dimension=1, tiled=True)
        solved_list.append(result)
    first_x = solved_list[0]
    second_x = solved_list[1]
    return (jnp.stack([first_x, second_x]), pending)


def solution(mesh):
    return jax.shard_map(
        body,
        mesh=mesh,
        in_specs=(
            P("prow", "pcol"),
            P("pcol", "prow"),
            P("prow", "pcol"),
            P(None, "prow", "pcol"),
            P(None, "pcol", None),
        ),
        out_specs=(P(None, "pcol", None), P("prow", "pcol")),
        check_vma=False,
    )
```

profile of v0, /device:TPU:29, one launch (start us, length us, event | category | flops | bytes accessed | tf_op | source)
XLA Modules:
  0.0 333.4 jit_solution(1964586816087864626)
XLA Ops:
  7.2 0.0 copy-start.1
  7.2 0.0 all-gather.2.cloned.1.call-start
  7.2 0.7 all-gather.2.cloned.1.call-update
  7.9 0.0 copy-start.2
  7.9 0.0 copy-start
  7.9 0.0 reduce-scatter.4.cloned.1.call-start
  8.0 46.8 %all-gather.2.cloned.1.call-done = bf16[6144,256]{0,1:T(8,128)(2,1)} async-done(((bf16[6144,16]{0,1:T(8,128)(2,1)}), bf16[6144,256]{0,1:T(8,128)(2,1)}) %all-gather.2.cloned.1.call-update) | async-done | bytes 3145744 | tf_op jit(solution)/shard_map/all_gather | solution.py:18
  54.8 9.9 %fusion.20 = f32[1024,256]{1,0:T(8,128)} fusion(bf16[1024,6144]{1,0:T(8,128)(2,1)} %param.5, bf16[6144,256]{0,1:T(8,128)(2,1)} %all-gather.2.cloned.1.call-done), kind=kOutput, calls=%fused_computation.29 | convolution fusion | flops 3221225472 | bytes 16777216 | tf_op jit(solution)/shard_map/dot_general | solution.py:16
  64.7 0.0 reduce-scatter.4.cloned.1.call-update
  64.7 0.0 all-reduce.3.cloned.1.call-start
  64.7 20.9 %reduce-scatter.4.cloned.1.call-done = f32[1024,128]{1,0:T(8,128)} async-done(((f32[1024,256]{1,0:T(8,128)}), f32[1024,128]{1,0:T(8,128)}) %reduce-scatter.4.cloned.1.call-update) | async-done | bytes 524304 | tf_op jit(solution)/shard_map/reduce_scatter | solution.py:28
  85.6 0.0 copy-done.1
  85.6 1.1 convert_subtract_fusion
  86.8 5.1 %all_gather.10 = bf16[512,256]{1,0:T(8,128)(2,1)S(1)} all-gather(bf16[512,128]{1,0:T(8,128)(2,1)S(1)} %slice.47), channel_id=1, replica_groups=mesh['prow'=16,'pcol'=2] {'pcol'}, dimensions={1}, use_global_device_ids=true | all-gather | bytes 393216 | tf_op jit(solution)/shard_map/all_gather | solution.py:34
  91.8 0.0 copy-done.2
  91.8 0.9 fusion.1
  92.8 0.0 all-reduce.3.cloned.1.call-update
  92.8 0.0 reduce-scatter.6.cloned.1.call-start
  92.9 86.5 %all-reduce.3.cloned.1.call-done = bf16[256,256]{0,1:T(8,128)(2,1)} async-done(((bf16[256,256]{0,1:T(8,128)(2,1)}), bf16[256,256]{0,1:T(8,128)(2,1)}) %all-reduce.3.cloned.1.call-update) | async-done | bytes 131088 | tf_op jit(solution)/shard_map/psum | solution.py:9
  179.3 0.0 copy-done
  179.4 2.2 fusion.5
  181.6 0.0 reduce-scatter.6.cloned.1.call-update
  181.6 0.0 all-reduce.5.cloned.1.call-start
  181.7 23.5 %reduce-scatter.6.cloned.1.call-done = f32[1024,128]{1,0:T(8,128)} async-done(((f32[1024,256]{1,0:T(8,128)}), f32[1024,128]{1,0:T(8,128)}) %reduce-scatter.6.cloned.1.call-update) | async-done | bytes 524304 | tf_op jit(solution)/shard_map/reduce_scatter | solution.py:43
  205.2 1.1 sub.10
  206.3 5.1 %all_gather.11 = bf16[512,256]{1,0:T(8,128)(2,1)S(1)} all-gather(bf16[512,128]{1,0:T(8,128)(2,1)S(1)} %slice.46), channel_id=1, replica_groups=mesh['prow'=16,'pcol'=2] {'pcol'}, dimensions={1}, use_global_device_ids=true | all-gather | bytes 393216 | tf_op jit(solution)/shard_map/all_gather | solution.py:34
  211.4 0.9 fusion.3
  212.3 0.0 all-reduce.5.cloned.1.call-update
  212.3 0.0 reduce-scatter.8.cloned.1.call-start
  212.4 86.4 %all-reduce.5.cloned.1.call-done = bf16[256,256]{0,1:T(8,128)(2,1)} async-done(((bf16[256,256]{0,1:T(8,128)(2,1)}), bf16[256,256]{0,1:T(8,128)(2,1)}) %all-reduce.5.cloned.1.call-update) | async-done | bytes 131088 | tf_op jit(solution)/shard_map/psum | solution.py:9
  298.8 2.2 fusion.4
  301.1 0.0 reduce-scatter.8.cloned.1.call-update
  301.1 1.0 pad_maximum_fusion
  302.1 0.8 copy.7
  302.9 21.7 %reduce-scatter.8.cloned.1.call-done = f32[1024,128]{1,0:T(8,128)} async-done(((f32[1024,256]{1,0:T(8,128)}), f32[1024,128]{1,0:T(8,128)}) %reduce-scatter.8.cloned.1.call-update) | async-done | bytes 524304 | tf_op jit(solution)/shard_map/reduce_scatter | solution.py:43
  324.6 1.9 sub.11
  (4 shorter events, 0.0 us)
Async XLA Ops:
  7.2 78.5 %copy-start.1 = (bf16[1024,128]{1,0:T(8,128)(2,1)S(1)}, bf16[1024,128]{1,0:T(8,128)(2,1)}, u32[]{:S(2)}) copy-start(bf16[1024,128]{1,0:T(8,128)(2,1)} %param.7) | copy-start | bytes 786436
  7.2 47.6 %all-gather.2.cloned.1.call-start = ((), (), s32[]{:S(2)}) async-start(), calls=%async_computation.3 | async-start | bytes 3342336 | tf_op jit(solution)/shard_map/all_gather | solution.py:18
  7.9 83.9 %copy-start.2 = (bf16[2,256,512]{2,1,0:T(8,128)(2,1)S(1)}, bf16[2,256,512]{2,1,0:T(8,128)(2,1)}, u32[]{:S(2)}) copy-start(bf16[2,256,512]{2,1,0:T(8,128)(2,1)} %param.9) | copy-start | bytes 1572868
  7.9 171.4 %copy-start = (bf16[2,1024,256]{2,1,0:T(8,128)(2,1)S(1)}, bf16[2,1024,256]{2,1,0:T(8,128)(2,1)}, u32[]{:S(2)}) copy-start(bf16[2,1024,256]{2,1,0:T(8,128)(2,1)} %param.8) | copy-start | bytes 3145732
  7.9 77.7 %reduce-scatter.4.cloned.1.call-start = ((), (), s32[]{:S(2)}) async-start(), calls=%async_computation.4 | async-start | bytes 1572864 | tf_op jit(solution)/shard_map/reduce_scatter | solution.py:28
  64.7 114.7 %all-reduce.3.cloned.1.call-start = ((), (), s32[]{:S(2)}) async-start(), calls=%async_computation.5 | async-start | bytes 262144 | tf_op jit(solution)/shard_map/psum | solution.py:9
  92.8 112.4 %reduce-scatter.6.cloned.1.call-start = ((), (), s32[]{:S(2)}) async-start(), calls=%async_computation.6 | async-start | bytes 1572864 | tf_op jit(solution)/shard_map/reduce_scatter | solution.py:43
  181.6 117.2 %all-reduce.5.cloned.1.call-start = ((), (), s32[]{:S(2)}) async-start(), calls=%async_computation.7 | async-start | bytes 262144 | tf_op jit(solution)/shard_map/psum | solution.py:9
  212.3 112.3 %reduce-scatter.8.cloned.1.call-start = ((), (), s32[]{:S(2)}) async-start(), calls=%async_computation.8 | async-start | bytes 1572864 | tf_op jit(solution)/shard_map/reduce_scatter | solution.py:43
Sparse Core Ops, SparseCore 0:
  10.3 44.4 all-gather.1
  64.8 20.7 reduce-scatter.3
  92.9 86.3 all-reduce.2
  181.7 23.3 reduce-scatter.5
  212.4 86.3 all-reduce.4
  301.2 23.3 reduce-scatter.7
where the time goes:
time: 335 us; the launch traced here: 333 us
  waiting for transfers between devices  287 us (86%)
  matrix products  16.2 us (5%)
  between operations  14.2 us (4%)
  blocking collectives  10.2 us (3%)
  other arithmetic  5.08 us (2%)
    psum x2, waiting for transfers between devices, spread(): return lax.psum(block, axis)  173 us
    all_gather x1, waiting for transfers between devices, body(): lax.all_gather(prior_solution, 'prow', axis=1, tiled=True)  46.8 us
    reduce_scatter x2, waiting for transfers between devices, body(): lax.psum_scatter(update, 'pcol', scatter_dimension=1, tiled=True)  45.2 us
    reduce_scatter x1, waiting for transfers between devices, body(): lax.psum_scatter(partial_value, 'pcol', scatter_dimension=1, tiled=True)  20.9 us
    all_gather x2, blocking collectives, body(): gathered = lax.all_gather(diagonal, 'pcol', axis=1, tiled=True)  10.2 us
    dot_general x1, matrix products, body(): jnp.dot(prior_panel, lax.all_gather(prior_solution, 'prow', axis=1, tiled...  9.91 us
  transfers between devices with their start and end apart: 6, of which 6 were waited for; matrix products, arithmetic and copies ran while one was open for 1% of the time, Pallas kernels for 0%

commit v1 on v0

v1 whole, which is shorter than its diff:
```python
import functools

import jax
import jax.numpy as jnp
from jax import lax
from jax.experimental import pallas as pl
from jax.experimental.pallas import tpu as pltpu
from jax.sharding import PartitionSpec as P

CHUNKS = 8
MESH = pl.DeviceIdType.MESH
F32 = jnp.float32
BF16 = jnp.bfloat16


def kernel(
    R,
    C,
    panel_hbm,
    xt_hbm,
    right_hbm,
    new_hbm,
    inv_hbm,
    solved_ref,
    pending_ref,
    panel,
    xg,
    acc,
    right,
    news,
    invs,
    own,
    out_parts,
    in_parts,
    xs,
    sv,
    panel_sem,
    load_sem,
    ring_send,
    ring_recv,
    sib_send,
    sib_recv,
    news_send,
    news_recv,
    inv_send,
    inv_recv,
    part_send,
    part_recv,
    cast_send,
    cast_recv,
    sv_send,
    sv_recv,
):
    M, K = panel_hbm.shape
    n = R // 2
    Z = n // 2
    H = n // 2
    Q = CHUNKS
    Kc = K // Q
    half = M // 2
    w = right_hbm.shape[1]
    nb = inv_hbm.shape[1]
    C2 = C // 2

    row = lax.axis_index("prow")
    pc = lax.axis_index("pcol")
    core = lax.rem(row, 2)
    chip = row // 2
    y = lax.rem(chip, 2)
    z = chip // 2
    pos = jnp.where(y == 0, z, 2 * Z - 1 - z)

    def chip_at(p):
        p = lax.rem(p + 2 * n, n)
        return jnp.where(p < Z, 2 * p, 2 * (2 * Z - 1 - p) + 1)

    def ring_dev(p):
        return (chip_at(p) * 2 + core, pc)

    rightd, leftd = ring_dev(pos + 1), ring_dev(pos - 1)
    sibd = (chip * 2 + 1 - core, pc)
    others = [lax.rem(pc + d, C) for d in range(1, C)]

    load_x = pltpu.make_async_copy(xt_hbm, xg.at[chip, core], load_sem.at[0])
    load_x.start()
    load_new = pltpu.make_async_copy(new_hbm, news.at[pc], load_sem.at[1])
    load_inv = pltpu.make_async_copy(inv_hbm, invs.at[pc], load_sem.at[2])
    load_right = pltpu.make_async_copy(right_hbm, right, load_sem.at[3])

    def load_panel(k):
        cols = pl.ds(k * Kc, Kc)
        return pltpu.make_async_copy(panel_hbm.at[:, cols], panel.at[:, cols], panel_sem.at[k])

    barrier = pltpu.get_barrier_semaphore()
    peers = [rightd, leftd, sibd] + [(row, t) for t in others]
    for dev in peers:
        pl.semaphore_signal(barrier, inc=1, device_id=dev, device_id_type=MESH)

    for k in range(Q):
        load_panel(k).start()
    load_new.start()
    load_inv.start()
    load_right.start()
    load_x.wait()
    pl.semaphore_wait(barrier, len(peers))

    def hops(direction, k):
        return H if (k + direction) % 2 == 0 else H - 1

    def ring_copy(direction, k, h):
        source = chip_at(pos - h) if direction == 0 else chip_at(pos + h)
        slot = xg.at[source, core, :, pl.ds(k * Kc, Kc)]
        return pltpu.make_async_remote_copy(
            src_ref=slot, dst_ref=slot,
            send_sem=ring_send.at[direction, k, h], recv_sem=ring_recv.at[direction, k, h],
            device_id=rightd if direction == 0 else leftd, device_id_type=MESH)

    def ring_arrival(direction, k, h):
        source = chip_at(pos - h - 1) if direction == 0 else chip_at(pos + h + 1)
        slot = xg.at[source, core, :, pl.ds(k * Kc, Kc)]
        return pltpu.make_async_remote_copy(
            src_ref=slot, dst_ref=slot,
            send_sem=ring_send.at[direction, k, h], recv_sem=ring_recv.at[direction, k, h],
            device_id=rightd if direction == 0 else leftd, device_id_type=MESH)

    def sib_copy(k, mine):
        slot = xg.at[:, core if mine else 1 - core, :, pl.ds(k * Kc, Kc)]
        return pltpu.make_async_remote_copy(
            src_ref=slot, dst_ref=slot, send_sem=sib_send.at[k], recv_sem=sib_recv.at[k],
            device_id=sibd, device_id_type=MESH)

    def send_own(k):
        for direction in range(2):
            if hops(direction, k) > 0:
                ring_copy(direction, k, 0).start()

    new_pieces = [(0, half, half), (0, 0, half), (1, 0, M)]

    def new_copy(t, i, slot):
        s, lo, size = new_pieces[i]
        return pltpu.make_async_remote_copy(
            src_ref=new_hbm.at[s, pl.ds(lo, size)], dst_ref=news.at[slot, s, pl.ds(lo, size)],
            send_sem=news_send.at[t, i], recv_sem=news_recv.at[slot, i],
            device_id=(row, t), device_id_type=MESH)

    def inv_copy(t, slot):
        return pltpu.make_async_remote_copy(
            src_ref=inv_hbm, dst_ref=invs.at[slot],
            send_sem=inv_send.at[t], recv_sem=inv_recv.at[slot],
            device_id=(row, t), device_id_type=MESH)

    send_own(0)
    send_own(1)

    @pl.when(row == 0)
    def _():
        for t in others:
            inv_copy(t, pc).start()

    for t in others:
        new_copy(t, 0, pc).start()

    @pl.when(row > 0)
    def _():
        for t in others:
            new_copy(t, 1, pc).start()
            new_copy(t, 2, pc).start()

    def dot_rows(k, lo, size):
        cols = pl.ds(k * Kc, Kc)
        rows = pl.ds(lo, size)
        x = xg[:, :, :, cols].reshape(w * C, Kc)
        value = lax.dot_general(
            panel[rows, cols], x, (((1,), (1,)), ((), ())), preferred_element_type=F32)
        if k:
            value = acc[rows, :] + value
        return value

    def dot_chunk(k):
        load_panel(k).wait()
        sib_copy(k, False).wait_recv()
        acc[...] = dot_rows(k, 0, M)

    for step in range(1, Q + H):
        for h in range(H, 0, -1):
            k = step - h
            if 0 <= k < Q:
                for direction in range(2):
                    if h - 1 < hops(direction, k):
                        ring_arrival(direction, k, h - 1).wait_recv()
                    if h < hops(direction, k):
                        ring_copy(direction, k, h).start()
                if h == H:
                    sib_copy(k, True).start()
        if 2 <= step + 1 < Q:
            send_own(step + 1)
        if 0 <= step - H - 1 < Q - 1:
            dot_chunk(step - H - 1)

    def part_copy(t, i, slot):
        rows = pl.ds(i * half, half)
        return pltpu.make_async_remote_copy(
            src_ref=out_parts.at[t, rows], dst_ref=in_parts.at[slot, rows],
            send_sem=part_send.at[t, i], recv_sem=part_recv.at[slot, i],
            device_id=(row, t), device_id_type=MESH)

    load_panel(Q - 1).wait()
    sib_copy(Q - 1, False).wait_recv()
    for i in range(2):
        value = dot_rows(Q - 1, i * half, half)
        rows = pl.ds(i * half, half)
        for t in range(C):
            piece = value[:, t * w : (t + 1) * w]
            out_parts[t, rows, :] = piece.astype(BF16)

            @pl.when(pc == t)
            def _():
                own[rows, :] = piece

        for t in others:
            part_copy(t, i, pc).start()

    load_right.wait()
    load_new.wait()
    load_inv.wait()

    def start_rows(i):
        rows = pl.ds(i * half, half)
        value = right[rows, :].astype(F32) - own[rows, :]
        for t in others:
            part_copy(t, i, t).wait_recv()
            value = value - in_parts[t, rows, :].astype(F32)
        return value

    first_half = pl.ds(0, half)
    second_half = pl.ds(half, half)

    def cast_copy(way, s, part):
        slot = xs.at[s, pl.ds(part * C2, C2)]
        return pltpu.make_async_remote_copy(
            src_ref=slot, dst_ref=slot,
            send_sem=cast_send.at[way, s, part], recv_sem=cast_recv.at[s, part],
            device_id=(rightd, leftd, sibd)[way], device_id_type=MESH)

    to_right = (core == 0) & (pos < n // 2)
    to_left = (core == 0) & ((pos == 0) | (pos > n // 2 + 1))
    to_sib = core == 0

    def cast_on(s, part, act):
        for way, flag in enumerate((to_right, to_left, to_sib)):
            @pl.when(flag)
            def _():
                act(cast_copy(way, s, part))

    def sv_copy(t, s, slot):
        return pltpu.make_async_remote_copy(
            src_ref=xs.at[s, t], dst_ref=sv.at[slot, s],
            send_sem=sv_send.at[t, s], recv_sem=sv_recv.at[slot, s],
            device_id=(row, t), device_id_type=MESH)

    def share(s):
        for t in others:
            sv_copy(t, s, pc).start()
        sv[pc, s] = xs[s, pc]

    def product(s, rows):
        total = None
        for c in range(C):
            term = jnp.dot(news[c, s, rows, :], xs[s, c], preferred_element_type=F32)
            total = term if total is None else total + term
        return total

    def solve(s, block):
        for part in range(2):
            for c in range(part * C2, (part + 1) * C2):
                xs[s, c] = jnp.dot(invs[c, s], block, preferred_element_type=F32).astype(BF16)
            cast_on(s, part, lambda copy: copy.start())

    @pl.when(row == 0)
    def _():
        for t in others:
            inv_copy(t, t).wait_recv()
        first = start_rows(0)
        solve(0, first.astype(BF16))
        pending_ref[first_half, :] = first
        for t in others:
            new_copy(t, 0, t).wait_recv()
        second = start_rows(1) - product(0, second_half)
        solve(1, second.astype(BF16))
        pending_ref[second_half, :] = second
        share(0)
        share(1)

    @pl.when(row > 0)
    def _():
        pending_ref[first_half, :] = start_rows(0)
        pending_ref[second_half, :] = start_rows(1)
        for t in others:
            for i in range(3):
                new_copy(t, i, t).wait_recv()
        for s in range(2):
            for part in range(2):
                cast_copy(0, s, part).wait_recv()
                cast_on(s, part, lambda copy: copy.start())
            share(s)
            pending_ref[...] = pending_ref[...] - product(s, pl.ds(0, M))

    for s in range(2):
        for t in others:
            sv_copy(t, s, t).wait_recv()
        solved_ref[s] = jnp.concatenate([sv[c, s] for c in range(C)], axis=1)

    for k in range(Q):
        for direction in range(2):
            for h in range(hops(direction, k)):
                ring_copy(direction, k, h).wait_send()
        sib_copy(k, True).wait_send()
    for t in others:
        new_copy(t, 0, pc).wait_send()
        for i in range(2):
            part_copy(t, i, pc).wait_send()
            sv_copy(t, i, pc).wait_send()

    @pl.when(row == 0)
    def _():
        for t in others:
            inv_copy(t, pc).wait_send()

    @pl.when(row > 0)
    def _():
        for t in others:
            new_copy(t, 1, pc).wait_send()
            new_copy(t, 2, pc).wait_send()

    for s in range(2):
        for part in range(2):
            cast_on(s, part, lambda copy: copy.wait_send())


def body(R, C, prior_panel, prior_solution, right_side, new_panel, inverses):
    M, K = prior_panel.shape
    r = prior_solution.shape[1]
    w = right_side.shape[1]
    nb, NB = inverses.shape[1:]
    assert M == 2 * NB and w * C == r * R and R % 4 == 0 and C % 2 == 0
    Q, H = CHUNKS, R // 4
    dma = pltpu.SemaphoreType.DMA
    any_spec = pl.BlockSpec(memory_space=pl.ANY)
    vmem_spec = pl.BlockSpec(memory_space=pltpu.VMEM)
    return pl.pallas_call(
        functools.partial(kernel, R, C),
        out_shape=(
            jax.ShapeDtypeStruct((2, nb, w * C), BF16),
            jax.ShapeDtypeStruct((M, w), F32),
        ),
        in_specs=[any_spec] * 5,
        out_specs=(vmem_spec, vmem_spec),
        scratch_shapes=[
            pltpu.VMEM((M, K), BF16),
            pltpu.VMEM((R // 2, 2, r, K), BF16),
            pltpu.VMEM((M, w * C), F32),
            pltpu.VMEM((M, w), BF16),
            pltpu.VMEM((C, 2, M, NB // C), BF16),
            pltpu.VMEM((C, 2, nb, NB), BF16),
            pltpu.VMEM((M, w), F32),
            pltpu.VMEM((C, M, w), BF16),
            pltpu.VMEM((C, M, w), BF16),
            pltpu.VMEM((2, C, nb, w), BF16),
            pltpu.VMEM((C, 2, nb, w), BF16),
            dma((Q,)),
            dma((4,)),
            dma((2, Q, H)),
            dma((2, Q, H)),
            dma((Q,)),
            dma((Q,)),
            dma((C, 3)),
            dma((C, 3)),
            dma((C,)),
            dma((C,)),
            dma((C, 2)),
            dma((C, 2)),
            dma((3, 2, 2)),
            dma((2, 2)),
            dma((C, 2)),
            dma((C, 2)),
        ],
        compiler_params=pltpu.CompilerParams(
            collective_id=0, has_side_effects=True, vmem_limit_bytes=50 * 2**20
        ),
    )(prior_panel, prior_solution.T, right_side, new_panel, inverses)


def solution(mesh):
    return jax.shard_map(
        functools.partial(body, mesh.shape["prow"], mesh.shape["pcol"]),
        mesh=mesh,
        in_specs=(
            P("prow", "pcol"),
            P("pcol", "prow"),
            P("prow", "pcol"),
            P(None, "prow", "pcol"),
            P(None, "pcol", None),
        ),
        out_specs=(P(None, "pcol", None), P("prow", "pcol")),
        check_vma=False,
    )
```

time: 335 us -> 72.4 us (0.22)
  waiting for transfers between devices: 287 us -> 0 us
  Pallas kernels: 0 us -> 65.8 us
  matrix products: 16.2 us -> 0 us
  between operations: 14.2 us -> 0.65 us
  blocking collectives: 10.2 us -> 0 us
  other arithmetic: 5.08 us -> 0 us
  local copies, waits for them, and re-layouts: 0.89 us -> 5.63 us
    psum x2 -> x0, waiting for transfers between devices: 173 us -> none  [spread(): return lax.psum(block, axis)]
    reduce_scatter x3 -> x0, waiting for transfers between devices: 66.1 us -> none  [the longest x2 45.2 us: body(): lax.psum_scatter(update, 'pcol', scatter_dimension=1, tiled=True)]
    pallas_call x0 -> x1, Pallas kernels: none -> 65.8 us  [body(): pl.pallas_call(functools.partial(kernel, R, C), out_shape=(jax.ShapeDtype...]
    all_gather x1 -> x0, waiting for transfers between devices: 46.8 us -> none  [body(): lax.all_gather(prior_solution, 'prow', axis=1, tiled=True)]
    dot_general x5 -> x0, matrix products: 16.2 us -> none  [the longest x1 9.91 us: body(): jnp.dot(prior_panel, lax.all_gather(prior_solution, 'prow', axis=1, tiled...]
    all_gather x2 -> x0, blocking collectives: 10.2 us -> none  [body(): gathered = lax.all_gather(diagonal, 'pcol', axis=1, tiled=True)]
    unnamed x7 -> x10, local copies, waits for them, and re-layouts: 0.85 us -> 5.63 us
    sub x3 -> x0, other arithmetic: 4.07 us -> none  [the longest x2 2.98 us: body(): pending - lax.psum_scatter(update, 'pcol', scatter_dimension=1, tiled=True)]
  transfers between devices with their start and end apart: 6 -> 0, of which waited for: 6 -> 0; matrix products, arithmetic and copies ran while one was open for 1% -> 0% of each run, Pallas kernels for 0% -> 0%
where the time goes in v1:
time: 72.4 us; the launch traced here: 72.1 us
  Pallas kernels  65.8 us (91%)
  local copies, waits for them, and re-layouts  5.63 us (8%)
    pallas_call x1, Pallas kernels, body(): pl.pallas_call(functools.partial(kernel, R, C), out_shape=(jax.ShapeDtype...  65.8 us
    unnamed x10, local copies, waits for them, and re-layouts  5.63 us

profile of v1, /device:TPU:29, one launch (start us, length us, event | category | flops | bytes accessed | tf_op | source)
XLA Modules:
  0.0 72.1 jit_solution(2551358082090360482)
XLA Ops:
  0.6 0.0 copy-start
  0.6 1.2 %copy-done = bf16[2,1024,256]{2,1,0:T(8,128)(2,1)S(1)} copy-done((bf16[2,1024,256]{2,1,0:T(8,128)(2,1)S(1)}, bf16[2,1024,256]{2,1,0:T(8,128)(2,1)}, u32[]{:S(2)}) %copy-start) | copy-done | bytes 1048600
  1.9 0.0 copy-start.1
  1.9 1.0 %copy-done.1 = bf16[2,256,512]{2,1,0:T(8,128)(2,1)S(1)} copy-done((bf16[2,256,512]{2,1,0:T(8,128)(2,1)S(1)}, bf16[2,256,512]{2,1,0:T(8,128)(2,1)}, u32[]{:S(2)}) %copy-start.1) | copy-done | bytes 524312
  2.9 0.0 copy-start.2
  2.9 0.9 %copy-done.2 = bf16[1024,128]{1,0:T(8,128)(2,1)S(1)} copy-done((bf16[1024,128]{1,0:T(8,128)(2,1)S(1)}, bf16[1024,128]{1,0:T(8,128)(2,1)}, u32[]{:S(2)}) %copy-start.2) | copy-done | bytes 262168
  3.8 0.0 copy-start.3
  3.9 0.9 %copy-done.3 = bf16[6144,16]{0,1:T(8,128)(2,1)S(1)} copy-done((bf16[6144,16]{0,1:T(8,128)(2,1)S(1)}, bf16[6144,16]{0,1:T(8,128)(2,1)}, u32[]{:S(2)}) %copy-start.3) | copy-done | bytes 196632
  4.8 65.8 %shard_map.68 = (bf16[2,256,256]{2,1,0:T(8,128)(2,1)S(1)}, f32[1024,128]{1,0:T(8,128)S(1)}) custom-call(bf16[1024,6144]{1,0:T(8,128)(2,1)} %panel_hbm.1, bf16[16,6144]{1,0:T(8,128)(2,1)S(1)} %bitcast.1, bf16[1024,128]{1,0:T(8,128)(2,1)S(1)} %copy-done.2, bf16[2,1024,256]{2,1,0:T(8,128)(2,1)S(1)} %copy-done, bf16[2,256,512]{2,1,0:T(8,128)(2,1)S(1)} %copy-done.1), custom_call_target="tpu_custom_call" | custom-call | tf_op jit(solution)/shard_map/pallas_call | solution.py:350
  70.6 0.7 copy.9
  71.3 0.8 %copy.10 = f32[1024,128]{1,0:T(8,128)} copy(f32[1024,128]{1,0:T(8,128)S(1)} %get-tuple-element.5) | data formatting | bytes 1048576
Async XLA Ops:
  0.6 1.2 %copy-start = (bf16[2,1024,256]{2,1,0:T(8,128)(2,1)S(1)}, bf16[2,1024,256]{2,1,0:T(8,128)(2,1)}, u32[]{:S(2)}) copy-start(bf16[2,1024,256]{2,1,0:T(8,128)(2,1)} %new_hbm.1) | copy-start | bytes 3145732
  1.9 1.0 %copy-start.1 = (bf16[2,256,512]{2,1,0:T(8,128)(2,1)S(1)}, bf16[2,256,512]{2,1,0:T(8,128)(2,1)}, u32[]{:S(2)}) copy-start(bf16[2,256,512]{2,1,0:T(8,128)(2,1)} %inv_hbm.1) | copy-start | bytes 1572868
  2.9 0.9 %copy-start.2 = (bf16[1024,128]{1,0:T(8,128)(2,1)S(1)}, bf16[1024,128]{1,0:T(8,128)(2,1)}, u32[]{:S(2)}) copy-start(bf16[1024,128]{1,0:T(8,128)(2,1)} %right_hbm.1) | copy-start | bytes 786436
  3.8 0.9 %copy-start.3 = (bf16[6144,16]{0,1:T(8,128)(2,1)S(1)}, bf16[6144,16]{0,1:T(8,128)(2,1)}, u32[]{:S(2)}) copy-start(bf16[6144,16]{0,1:T(8,128)(2,1)} %param.6) | copy-start | bytes 589828

commit v2 on v1

--- a/solution.py
+++ b/solution.py
@@ -149,8 +149,8 @@
             send_sem=inv_send.at[t], recv_sem=inv_recv.at[slot],
             device_id=(row, t), device_id_type=MESH)
 
-    send_own(0)
-    send_own(1)
+    for k in range(Q):
+        send_own(k)
 
     @pl.when(row == 0)
     def _():
@@ -181,21 +181,17 @@
         sib_copy(k, False).wait_recv()
         acc[...] = dot_rows(k, 0, M)
 
-    for step in range(1, Q + H):
-        for h in range(H, 0, -1):
-            k = step - h
-            if 0 <= k < Q:
-                for direction in range(2):
-                    if h - 1 < hops(direction, k):
-                        ring_arrival(direction, k, h - 1).wait_recv()
-                    if h < hops(direction, k):
-                        ring_copy(direction, k, h).start()
-                if h == H:
-                    sib_copy(k, True).start()
-        if 2 <= step + 1 < Q:
-            send_own(step + 1)
-        if 0 <= step - H - 1 < Q - 1:
-            dot_chunk(step - H - 1)
+    for h in range(1, H + 1):
+        for k in range(Q):
+            for direction in range(2):
+                if h - 1 < hops(direction, k):
+                    ring_arrival(direction, k, h - 1).wait_recv()
+                if h < hops(direction, k):
+                    ring_copy(direction, k, h).start()
+            if h == H:
+                sib_copy(k, True).start()
+                if k > 0:
+                    dot_chunk(k - 1)
 
     def part_copy(t, i, slot):
         rows = pl.ds(i * half, half)
@@ -217,8 +213,10 @@
             def _():
                 own[rows, :] = piece
 
-        for t in others:
-            part_copy(t, i, pc).start()
+        @pl.when(row != 1)
+        def _():
+            for t in others:
+                part_copy(t, i, pc).start()
 
     load_right.wait()
     load_new.wait()
@@ -293,17 +291,28 @@
 
     @pl.when(row > 0)
     def _():
-        pending_ref[first_half, :] = start_rows(0)
-        pending_ref[second_half, :] = start_rows(1)
         for t in others:
             for i in range(3):
                 new_copy(t, i, t).wait_recv()
-        for s in range(2):
-            for part in range(2):
-                cast_copy(0, s, part).wait_recv()
-                cast_on(s, part, lambda copy: copy.start())
-            share(s)
-            pending_ref[...] = pending_ref[...] - product(s, pl.ds(0, M))
+        for part in range(2):
+            cast_copy(0, 0, part).wait_recv()
+            cast_on(0, part, lambda copy: copy.start())
+
+        @pl.when(row == 1)
+        def _():
+            for i in range(2):
+                for t in others:
+                    part_copy(t, i, pc).start()
+
+        share(0)
+        acc[:, :w] = product(0, pl.ds(0, M))
+        pending_ref[first_half, :] = start_rows(0) - acc[first_half, :w]
+        pending_ref[second_half, :] = start_rows(1) - acc[second_half, :w]
+        for part in range(2):
+            cast_copy(0, 1, part).wait_recv()
+            cast_on(1, part, lambda copy: copy.start())
+        share(1)
+        pending_ref[...] = pending_ref[...] - product(1, pl.ds(0, M))
 
     for s in range(2):
         for t in others:
@@ -345,7 +354,7 @@
     assert M == 2 * NB and w * C == r * R and R % 4 == 0 and C % 2 == 0
     Q, H = CHUNKS, R // 4
     dma = pltpu.SemaphoreType.DMA
-    any_spec = pl.BlockSpec(memory_space=pl.ANY)
+    any_spec = pl.BlockSpec(memory_space=pltpu.HBM)
     vmem_spec = pl.BlockSpec(memory_space=pltpu.VMEM)
     return pl.pallas_call(
         functools.partial(kernel, R, C),
@@ -385,7 +394,7 @@
             dma((C, 2)),
         ],
         compiler_params=pltpu.CompilerParams(
-            collective_id=0, has_side_effects=True, vmem_limit_bytes=50 * 2**20
+            collective_id=0, has_side_effects=True, vmem_limit_bytes=62 * 2**20
         ),
     )(prior_panel, prior_solution.T, right_side, new_panel, inverses)
 

time: 72.4 us -> 55.1 us (0.76)
  Pallas kernels: 65.8 us -> 50.7 us
  local copies, waits for them, and re-layouts: 5.63 us -> 3.54 us
    pallas_call x1, Pallas kernels: 65.8 us -> 50.7 us  [body(): pl.pallas_call(functools.partial(kernel, R, C), out_shape=(jax.ShapeDtype...]
    unnamed x10 -> x2, local copies, waits for them, and re-layouts: 5.63 us -> 3.54 us
where the time goes in v2:
time: 55.1 us; the launch traced here: 54.9 us
  Pallas kernels  50.7 us (92%)
  local copies, waits for them, and re-layouts  3.54 us (6%)
  between operations  0.64 us (1%)
    pallas_call x1, Pallas kernels, body(): pl.pallas_call(functools.partial(kernel, R, C), out_shape=(jax.ShapeDtype...  50.7 us
    unnamed x2, local copies, waits for them, and re-layouts  3.54 us

profile of v2, /device:TPU:29, one launch (start us, length us, event | category | flops | bytes accessed | tf_op | source)
XLA Modules:
  0.0 54.9 jit_solution(18157952073111604425)
XLA Ops:
  0.6 50.7 %shard_map.68 = (bf16[2,256,256]{2,1,0:T(8,128)(2,1)}, f32[1024,128]{1,0:T(8,128)}) custom-call(bf16[1024,6144]{1,0:T(8,128)(2,1)} %panel_hbm.1, bf16[16,6144]{1,0:T(8,128)(2,1)} %bitcast.1, bf16[1024,128]{1,0:T(8,128)(2,1)} %right_hbm.1, bf16[2,1024,256]{2,1,0:T(8,128)(2,1)} %new_hbm.1, bf16[2,256,512]{2,1,0:T(8,128)(2,1)} %inv_hbm.1), custom_call_target="tpu_custom_call" | custom-call | tf_op jit(solution)/shard_map/pallas_call | solution.py:359
  51.4 1.7 %copy.9 = bf16[2,256,256]{2,1,0:T(8,128)(2,1)} copy(bf16[2,256,256]{2,1,0:T(8,128)(2,1)} %get-tuple-element.4) | data formatting | bytes 524288
  53.0 1.9 %copy.10 = f32[1024,128]{1,0:T(8,128)} copy(f32[1024,128]{1,0:T(8,128)} %get-tuple-element.5) | data formatting | bytes 1048576

commit v3 on v2

--- a/solution.py
+++ b/solution.py
@@ -7,7 +7,7 @@
 from jax.experimental.pallas import tpu as pltpu
 from jax.sharding import PartitionSpec as P
 
-CHUNKS = 8
+CHUNKS = 3
 MESH = pl.DeviceIdType.MESH
 F32 = jnp.float32
 BF16 = jnp.bfloat16

time: 55.1 us -> 52.5 us (0.953)
  Pallas kernels: 50.7 us -> 48.2 us
    pallas_call x1, Pallas kernels: 50.7 us -> 48.2 us  [body(): pl.pallas_call(functools.partial(kernel, R, C), out_shape=(jax.ShapeDtype...]
where the time goes in v3:
time: 52.5 us; the launch traced here: 52.4 us
  Pallas kernels  48.2 us (92%)
  local copies, waits for them, and re-layouts  3.54 us (7%)
  between operations  0.64 us (1%)
    pallas_call x1, Pallas kernels, body(): pl.pallas_call(functools.partial(kernel, R, C), out_shape=(jax.ShapeDtype...  48.2 us
    unnamed x2, local copies, waits for them, and re-layouts  3.54 us

profile of v3, /device:TPU:29, one launch (start us, length us, event | category | flops | bytes accessed | tf_op | source)
XLA Modules:
  0.0 52.4 jit_solution(16821222717319568269)
XLA Ops:
  0.6 48.2 %shard_map.68 = (bf16[2,256,256]{2,1,0:T(8,128)(2,1)}, f32[1024,128]{1,0:T(8,128)}) custom-call(bf16[1024,6144]{1,0:T(8,128)(2,1)} %panel_hbm.1, bf16[16,6144]{1,0:T(8,128)(2,1)} %bitcast.1, bf16[1024,128]{1,0:T(8,128)(2,1)} %right_hbm.1, bf16[2,1024,256]{2,1,0:T(8,128)(2,1)} %new_hbm.1, bf16[2,256,512]{2,1,0:T(8,128)(2,1)} %inv_hbm.1), custom_call_target="tpu_custom_call" | custom-call | tf_op jit(solution)/shard_map/pallas_call | solution.py:359
  48.8 1.7 %copy.9 = bf16[2,256,256]{2,1,0:T(8,128)(2,1)} copy(bf16[2,256,256]{2,1,0:T(8,128)(2,1)} %get-tuple-element.4) | data formatting | bytes 524288
  50.5 1.9 %copy.10 = f32[1024,128]{1,0:T(8,128)} copy(f32[1024,128]{1,0:T(8,128)} %get-tuple-element.5) | data formatting | bytes 1048576
